TPU v7x, 256 devices: a whole 4x4x8 slice. The times are simulated.
256 devices in a mesh: row: 16 (over z, y_lo), col: 16 (over x, y_hi, core).
Axes of the slice: x: 4, y: 4 (y_hi: 2, y_lo: 2; y = y_hi * 2 + y_lo), z: 8, core: 2. Of those that a mesh axis runs over, the one named last changes fastest.
Arguments:
- features: bfloat16 [768, 8192], P('col', 'row'), may hold values from -6 to 6
- gate_weight: bfloat16 [8192, 14336], P('row', 'col'), may hold values from -0.0625 to 0.0625
- up_weight: bfloat16 [8192, 14336], P('row', 'col'), may hold values from -0.0625 to 0.0625
- down_weight: bfloat16 [14336, 8192], P('col', 'row'), may hold values from -0.046875 to 0.046875
- cotangent: bfloat16 [768, 8192], P('col', 'row'), may hold values from -6 to 6
Outputs:
- output: float32 [768, 8192], P('col', 'row')
- input_grad: float32 [768, 8192], P('col', 'row')
- gate_wgrad: float32 [8192, 14336], P('row', 'col')
- up_wgrad: float32 [8192, 14336], P('row', 'col')
- down_wgrad: float32 [14336, 8192], P('col', 'row')
All inputs are finite; a program needn't handle non-finite values.
Results may differ from a plain program's by a relative error of at most 0.0029.
Values may be sent and summed in bfloat16 or wider, within the bound.
A program may use at most 64 MiB of HBM per device.

v0:
```python
import jax
import jax.numpy as jnp
from jax import lax
from jax.sharding import PartitionSpec as P


def times_transposed(left, right):
    return lax.dot_general(
        left, right, (((1,), (1,)), ((), ())), preferred_element_type=jnp.float32
    )


def over_tokens(left, right):
    return lax.dot_general(
        left, right, (((0,), (0,)), ((), ())), preferred_element_type=jnp.float32
    )


def body(features, gate_weight, up_weight, down_weight, cotangent):
    hidden_cols = gate_weight.shape[1]
    both_weights = jnp.concatenate([gate_weight, up_weight], axis=1)
    gathered = lax.all_gather(features, "col", axis=0, tiled=True)
    cot_all = lax.all_gather(cotangent, "col", axis=0, tiled=True)
    block = gathered
    pre_acts = lax.psum_scatter(
        jnp.dot(block, both_weights, preferred_element_type=jnp.float32),
        "row",
        scatter_dimension=0,
        tiled=True,
    )
    block = cot_all
    hid_grad = lax.psum_scatter(
        times_transposed(block, down_weight), "row", scatter_dimension=0, tiled=True
    )
    gate_pre = pre_acts[:, :hidden_cols]
    up_pre = pre_acts[:, hidden_cols:]
    sig = jax.nn.sigmoid(gate_pre)
    silu_gate = gate_pre * sig
    hidden = (silu_gate * up_pre).astype(jnp.bfloat16)
    gate_grad = (hid_grad * up_pre * sig * (1.0 + gate_pre * (1.0 - sig))).astype(jnp.bfloat16)
    up_grad = (hid_grad * silu_gate).astype(jnp.bfloat16)
    hidden_all = lax.all_gather(hidden, "row", axis=0, tiled=True)
    block = hidden_all
    output = lax.psum_scatter(
        jnp.dot(block, down_weight, preferred_element_type=jnp.float32),
        "col",
        scatter_dimension=0,
        tiled=True,
    )
    gate_all, up_all = (
        lax.all_gather(gate_grad, "row", axis=0, tiled=True),
        lax.all_gather(up_grad, "row", axis=0, tiled=True),
    )
    input_grad = lax.psum_scatter(
        times_transposed(gate_all, gate_weight) + times_transposed(up_all, up_weight),
        "col",
        scatter_dimension=0,
        tiled=True,
    )
    gate_wgrad = over_tokens(gathered, gate_all)
    up_wgrad = over_tokens(gathered, up_all)
    down_wgrad = over_tokens(hidden_all, cot_all)
    return (output, input_grad, gate_wgrad, up_wgrad, down_wgrad)


def solution(mesh):
    in_specs = (P("col", "row"), P("row", "col"), P("row", "col"), P("col", "row"), P("col", "row"))
    out_specs = (
        P("col", "row"),
        P("col", "row"),
        P("row", "col"),
        P("row", "col"),
        P("col", "row"),
    )
    return jax.shard_map(body, mesh=mesh, in_specs=in_specs, out_specs=out_specs, check_vma=False)
```

profile of v0, /device:TPU:2, one launch (start us, length us, event | category | flops | bytes accessed | tf_op | source)
XLA Modules:
  0.0 629.4 jit_solution(1231802147683455028)
XLA Ops:
  7.2 0.0 copy-start
  7.2 0.0 reduce-scatter.15.cloned.1.call-start
  7.2 24.7 %all_gather.17 = bf16[768,512]{1,0:T(8,128)(2,1)S(1)} all-gather(bf16[48,512]{1,0:T(8,128)(2,1)} %param.9), channel_id=1, replica_groups=mesh['row'=16,'col'=16] {'col'}, dimensions={0}, use_global_device_ids=true | all-gather | bytes 835584 | tf_op jit(solution)/shard_map/all_gather | solution.py:23
  31.9 0.0 copy-done
  31.9 2.7 fusion.6
  34.6 0.0 copy-start.3
  34.6 0.0 copy-start.1
  34.6 0.0 reduce-scatter.15.cloned.1.call-update
  34.6 0.0 reduce-scatter.13.cloned.1.call-start
  34.7 0.7 copy-done.3
  35.4 25.4 %all_gather.15 = bf16[768,512]{1,0:T(8,128)(2,1)S(1)} all-gather(bf16[48,512]{1,0:T(8,128)(2,1)S(1)} %copy-done.3), channel_id=1, replica_groups=mesh['row'=16,'col'=16] {'col'}, dimensions={0}, use_global_device_ids=true | all-gather | bytes 835584 | tf_op jit(solution)/shard_map/all_gather | solution.py:22
  60.8 0.0 copy-start.2
  60.8 0.9 copy-done.2
  61.6 0.0 copy-done.1
  61.6 5.3 convolution_bitcast_fusion
  66.9 6.1 copy.27
  73.1 0.0 reduce-scatter.13.cloned.1.call-update
  73.1 0.0 all-gather.6.cloned.1.call-start
  73.1 44.8 %reduce-scatter.15.cloned.1.call-done = f32[48,896]{1,0:T(8,128)} async-done(((f32[768,896]{1,0:T(8,128)}), f32[48,896]{1,0:T(8,128)}) %reduce-scatter.15.cloned.1.call-update) | async-done | bytes 172048 | tf_op jit(solution)/shard_map/reduce_scatter | solution.py:32
  118.0 126.3 %reduce-scatter.13.cloned.1.call-done = f32[48,1792]{1,0:T(8,128)} async-done(((f32[768,1792]{1,0:T(8,128)}), f32[48,1792]{1,0:T(8,128)}) %reduce-scatter.13.cloned.1.call-update) | async-done | bytes 344080 | tf_op jit(solution)/shard_map/reduce_scatter | solution.py:25
  244.3 1.9 multiply_convert_fusion
  246.1 0.0 all-gather.6.cloned.1.call-update
  246.1 0.0 all-gather.8.cloned.1.call-start
  246.2 0.5 all-gather.8.cloned.1.call-update
  246.7 0.0 all-gather.4.cloned.1.call-start
  246.8 0.5 all-gather.4.cloned.1.call-update
  247.3 0.0 reduce-scatter.11.cloned.1.call-start
  247.3 69.0 %all-gather.6.cloned.1.call-done = bf16[768,896]{1,0:T(8,128)(2,1)} async-done(((bf16[48,896]{1,0:T(8,128)(2,1)}), bf16[768,896]{1,0:T(8,128)(2,1)}) %all-gather.6.cloned.1.call-update) | async-done | bytes 1376272 | tf_op jit(solution)/shard_map/all_gather | solution.py:51
  316.3 2.6 fusion.7
  319.0 69.6 %all-gather.8.cloned.1.call-done = bf16[768,896]{1,0:T(8,128)(2,1)} async-done(((bf16[48,896]{1,0:T(8,128)(2,1)}), bf16[768,896]{1,0:T(8,128)(2,1)}) %all-gather.8.cloned.1.call-update) | async-done | bytes 1376272 | tf_op jit(solution)/shard_map/all_gather | solution.py:52
  388.6 3.7 convolution_add_fusion
  392.3 0.0 reduce-scatter.11.cloned.1.call-update
  392.4 0.0 reduce-scatter.9.cloned.1.call-start
  392.4 68.4 %all-gather.4.cloned.1.call-done = bf16[768,896]{1,0:T(8,128)(2,1)} async-done(((bf16[48,896]{1,0:T(8,128)(2,1)}), bf16[768,896]{1,0:T(8,128)(2,1)}) %all-gather.4.cloned.1.call-update) | async-done | bytes 1376272 | tf_op jit(solution)/shard_map/all_gather | solution.py:42
  460.8 3.5 fusion.5
  464.3 0.0 reduce-scatter.9.cloned.1.call-update
  464.3 2.5 convolution_bitcast_fusion.2
  466.8 1.7 copy.24
  468.5 2.4 convolution_bitcast_fusion.1
  470.9 1.7 copy.25
  472.6 3.5 fusion.8
  476.1 66.1 %reduce-scatter.11.cloned.1.call-done = f32[48,512]{1,0:T(8,128)} async-done(((f32[768,512]{1,0:T(8,128)}), f32[48,512]{1,0:T(8,128)}) %reduce-scatter.11.cloned.1.call-update) | async-done | bytes 98320 | tf_op jit(solution)/shard_map/reduce_scatter | solution.py:54
  542.2 80.4 %reduce-scatter.9.cloned.1.call-done = f32[48,512]{1,0:T(8,128)} async-done(((f32[768,512]{1,0:T(8,128)}), f32[48,512]{1,0:T(8,128)}) %reduce-scatter.9.cloned.1.call-update) | async-done | bytes 98320 | tf_op jit(solution)/shard_map/reduce_scatter | solution.py:44
Async XLA Ops:
  7.2 24.8 %copy-start = (bf16[896,512]{1,0:T(8,128)(2,1)S(1)}, bf16[896,512]{1,0:T(8,128)(2,1)}, u32[]{:S(2)}) copy-start(bf16[896,512]{1,0:T(8,128)(2,1)} %param.8) | copy-start | bytes 2752516
  7.2 110.8 %reduce-scatter.15.cloned.1.call-start = ((), (), s32[]{:S(2)}) async-start(), calls=%async_computation.10 | async-start | bytes 2924544 | tf_op jit(solution)/shard_map/reduce_scatter | solution.py:32
  34.6 0.8 copy-start.3
  34.6 27.0 %copy-start.1 = (bf16[512,896]{1,0:T(8,128)(2,1)S(1)}, bf16[512,896]{1,0:T(8,128)(2,1)}, u32[]{:S(2)}) copy-start(bf16[512,896]{1,0:T(8,128)(2,1)} %param.7) | copy-start | bytes 2752516
  34.6 209.6 %reduce-scatter.13.cloned.1.call-start = ((), (), s32[]{:S(2)}) async-start(), calls=%async_computation.9 | async-start | bytes 5849088 | tf_op jit(solution)/shard_map/reduce_scatter | solution.py:25
  60.8 0.9 copy-start.2
  73.1 243.3 %all-gather.6.cloned.1.call-start = ((), (), s32[]{:S(2)}) async-start(), calls=%async_computation.6 | async-start | bytes 1462272 | tf_op jit(solution)/shard_map/all_gather | solution.py:51
  246.1 142.5 %all-gather.8.cloned.1.call-start = ((), (), s32[]{:S(2)}) async-start(), calls=%async_computation.7 | async-start | bytes 1462272 | tf_op jit(solution)/shard_map/all_gather | solution.py:52
  246.7 214.1 %all-gather.4.cloned.1.call-start = ((), (), s32[]{:S(2)}) async-start(), calls=%async_computation.4 | async-start | bytes 1462272 | tf_op jit(solution)/shard_map/all_gather | solution.py:42
  247.3 294.9 %reduce-scatter.11.cloned.1.call-start = ((), (), s32[]{:S(2)}) async-start(), calls=%async_computation.8 | async-start | bytes 1671168 | tf_op jit(solution)/shard_map/reduce_scatter | solution.py:54
  392.4 230.2 %reduce-scatter.9.cloned.1.call-start = ((), (), s32[]{:S(2)}) async-start(), calls=%async_computation.5 | async-start | bytes 1671168 | tf_op jit(solution)/shard_map/reduce_scatter | solution.py:44
Sparse Core Ops, SparseCore 0:
  34.8 83.1 reduce-scatter.14
  120.7 123.4 reduce-scatter.12
  246.6 69.6 all-gather.5
  318.6 69.9 all-gather.7
  390.8 69.9 all-gather.3
  465.4 76.7 reduce-scatter.10
  546.9 75.5 reduce-scatter.8
where the time goes:
time: 630 us; the launch traced here: 629 us
  waiting for transfers between devices  526 us (83%)
  blocking collectives  50.1 us (8%)
  matrix products  26.1 us (4%)
  between operations  14.2 us (2%)
  local copies, waits for them, and re-layouts  11.1 us (2%)
    reduce_scatter x1, waiting for transfers between devices, body(): lax.psum_scatter(jnp.dot(block, both_weights, preferred_element_type=jnp....  126 us
    reduce_scatter x1, waiting for transfers between devices, body(): lax.psum_scatter(jnp.dot(block, down_weight, preferred_element_type=jnp.f...  80.4 us
    all_gather x1, waiting for transfers between devices, body(): lax.all_gather(up_grad, 'row', axis=0, tiled=True)  69.6 us
    all_gather x1, waiting for transfers between devices, body(): lax.all_gather(gate_grad, 'row', axis=0, tiled=True)  69 us
    all_gather x1, waiting for transfers between devices, body(): hidden_all = lax.all_gather(hidden, 'row', axis=0, tiled=True)  68.4 us
    reduce_scatter x1, waiting for transfers between devices, body(): lax.psum_scatter(times_transposed(gate_all, gate_weight) + times_transpos...  66.1 us
    reduce_scatter x1, waiting for transfers between devices, body(): lax.psum_scatter(times_transposed(block, down_weight), 'row', scatter_dim...  44.8 us
    all_gather x1, blocking collectives, body(): gathered = lax.all_gather(features, 'col', axis=0, tiled=True)  25.4 us
  transfers between devices with their start and end apart: 7, of which 7 were waited for; matrix products, arithmetic and copies ran while one was open for 5% of the time, Pallas kernels for 0%

commit v1 on v0

--- a/solution.py
+++ b/solution.py
@@ -19,8 +19,11 @@
 def body(features, gate_weight, up_weight, down_weight, cotangent):
     hidden_cols = gate_weight.shape[1]
     both_weights = jnp.concatenate([gate_weight, up_weight], axis=1)
-    gathered = lax.all_gather(features, "col", axis=0, tiled=True)
-    cot_all = lax.all_gather(cotangent, "col", axis=0, tiled=True)
+    gathered, cot_all = jnp.split(
+        lax.all_gather(jnp.concatenate([features, cotangent], axis=1), "col", axis=0, tiled=True),
+        [features.shape[1]],
+        axis=1,
+    )
     block = gathered
     pre_acts = lax.psum_scatter(
         jnp.dot(block, both_weights, preferred_element_type=jnp.float32),

time: 630 us -> 660 us (1.048)
  waiting for transfers between devices: 526 us -> 612 us
  blocking collectives: 50.1 us -> 0 us
  local copies, waits for them, and re-layouts: 11.1 us -> 3.02 us
    all_gather x0 -> x1, waiting for transfers between devices: none -> 56.9 us  [body(): lax.all_gather(jnp.concatenate([features, cotangent], axis=1), 'col', axi...]
    all_gather x2 -> x0, blocking collectives: 50.1 us -> none  [the longest x1 25.4 us: body(): gathered = lax.all_gather(features, 'col', axis=0, tiled=True)]
    reduce_scatter x1, waiting for transfers between devices: 44.8 us -> 70.5 us  [body(): lax.psum_scatter(times_transposed(block, down_weight), 'row', scatter_dim...]
    reduce_scatter x1, waiting for transfers between devices: 66.1 us -> 80.4 us  [body(): lax.psum_scatter(times_transposed(gate_all, gate_weight) + times_transpos...]
    reduce_scatter x1, waiting for transfers between devices: 80.4 us -> 68.5 us  [body(): lax.psum_scatter(jnp.dot(block, down_weight, preferred_element_type=jnp.f...]
    unnamed x11 -> x12, local copies, waits for them, and re-layouts: 11.1 us -> 3.02 us
  transfers between devices with their start and end apart: 7 -> 8, of which waited for: 7 -> 8; matrix products, arithmetic and copies ran while one was open for 5% -> 3% of each run, Pallas kernels for 0% -> 0%
where the time goes in v1:
time: 660 us
  waiting for transfers between devices  612 us (93%)
  matrix products  26.5 us (4%)
  between operations  14.2 us (2%)
    reduce_scatter x1, waiting for transfers between devices, body(): lax.psum_scatter(jnp.dot(block, both_weights, preferred_element_type=jnp....  128 us
    reduce_scatter x1, waiting for transfers between devices, body(): lax.psum_scatter(times_transposed(gate_all, gate_weight) + times_transpos...  80.4 us
    reduce_scatter x1, waiting for transfers between devices, body(): lax.psum_scatter(times_transposed(block, down_weight), 'row', scatter_dim...  70.5 us
    all_gather x1, waiting for transfers between devices, body(): lax.all_gather(up_grad, 'row', axis=0, tiled=True)  69.6 us
    all_gather x1, waiting for transfers between devices, body(): hidden_all = lax.all_gather(hidden, 'row', axis=0, tiled=True)  68.8 us
    all_gather x1, waiting for transfers between devices, body(): lax.all_gather(gate_grad, 'row', axis=0, tiled=True)  68.7 us
    reduce_scatter x1, waiting for transfers between devices, body(): lax.psum_scatter(jnp.dot(block, down_weight, preferred_element_type=jnp.f...  68.5 us
    all_gather x1, waiting for transfers between devices, body(): lax.all_gather(jnp.concatenate([features, cotangent], axis=1), 'col', axi...  56.9 us
  transfers between devices with their start and end apart: 8, of which 8 were waited for; matrix products, arithmetic and copies ran while one was open for 3% of the time, Pallas kernels for 0%

profile of v1, /device:TPU:2, one launch (start us, length us, event | category | flops | bytes accessed | tf_op | source)
XLA Modules:
  0.0 659.6 jit_solution(1900536358510791762)
XLA Ops:
  7.2 0.0 copy-start
  7.2 0.0 all-gather.5.cloned.1.call-start
  7.2 1.5 pad_maximum_fusion
  8.8 0.0 all-gather.5.cloned.1.call-update
  8.8 0.0 reduce-scatter.9.cloned.1.call-start
  8.8 56.9 %all-gather.5.cloned.1.call-done = bf16[768,1024]{1,0:T(8,128)(2,1)} async-done(((bf16[48,1024]{1,0:T(8,128)(2,1)}), bf16[768,1024]{1,0:T(8,128)(2,1)}) %all-gather.5.cloned.1.call-update) | async-done | bytes 1572880 | tf_op jit(solution)/shard_map/all_gather | solution.py:23
  65.8 0.0 copy-done
  65.8 3.7 fusion.6
  69.4 0.0 copy-start.1
  69.4 0.0 copy-start.2
  69.4 0.0 reduce-scatter.9.cloned.1.call-update
  69.5 0.0 reduce-scatter.5.cloned.1.call-start
  69.5 1.1 copy-done.1
  70.6 0.5 copy-done.2
  71.1 5.2 fusion
  76.3 0.0 reduce-scatter.5.cloned.1.call-update
  76.3 0.0 all-gather.7.cloned.1.call-start
  76.4 70.5 %reduce-scatter.9.cloned.1.call-done = f32[48,896]{1,0:T(8,128)} async-done(((f32[768,896]{1,0:T(8,128)}), f32[48,896]{1,0:T(8,128)}) %reduce-scatter.9.cloned.1.call-update) | async-done | bytes 172048 | tf_op jit(solution)/shard_map/reduce_scatter | solution.py:35
  146.9 127.6 %reduce-scatter.5.cloned.1.call-done = f32[48,1792]{1,0:T(8,128)} async-done(((f32[768,1792]{1,0:T(8,128)}), f32[48,1792]{1,0:T(8,128)}) %reduce-scatter.5.cloned.1.call-update) | async-done | bytes 344080 | tf_op jit(solution)/shard_map/reduce_scatter | solution.py:28
  274.5 1.9 multiply_convert_fusion
  276.4 0.0 all-gather.7.cloned.1.call-update
  276.4 0.0 all-gather.9.cloned.1.call-start
  276.4 0.5 all-gather.9.cloned.1.call-update
  277.0 0.0 all-gather.11.cloned.1.call-start
  277.0 0.5 all-gather.11.cloned.1.call-update
  277.5 0.0 reduce-scatter.7.cloned.1.call-start
  277.6 68.8 %all-gather.7.cloned.1.call-done = bf16[768,896]{1,0:T(8,128)(2,1)} async-done(((bf16[48,896]{1,0:T(8,128)(2,1)}), bf16[768,896]{1,0:T(8,128)(2,1)}) %all-gather.7.cloned.1.call-update) | async-done | bytes 1376272 | tf_op jit(solution)/shard_map/all_gather | solution.py:45
  346.4 3.5 fusion.15
  349.9 0.0 reduce-scatter.7.cloned.1.call-update
  349.9 0.0 reduce-scatter.11.cloned.1.call-start
  350.0 68.7 %all-gather.9.cloned.1.call-done = bf16[768,896]{1,0:T(8,128)(2,1)} async-done(((bf16[48,896]{1,0:T(8,128)(2,1)}), bf16[768,896]{1,0:T(8,128)(2,1)}) %all-gather.9.cloned.1.call-update) | async-done | bytes 1376272 | tf_op jit(solution)/shard_map/all_gather | solution.py:54
  418.7 2.6 fusion.16
  421.3 69.6 %all-gather.11.cloned.1.call-done = bf16[768,896]{1,0:T(8,128)(2,1)} async-done(((bf16[48,896]{1,0:T(8,128)(2,1)}), bf16[768,896]{1,0:T(8,128)(2,1)}) %all-gather.11.cloned.1.call-update) | async-done | bytes 1376272 | tf_op jit(solution)/shard_map/all_gather | solution.py:55
  490.9 3.5 convolution_add_fusion
  494.4 0.0 copy-start.3
  494.4 0.0 reduce-scatter.11.cloned.1.call-update
  494.4 1.4 copy-done.3
  495.8 0.0 copy-start.4
  495.8 3.6 fusion.4
  499.4 0.0 copy-done.4
  499.4 0.0 copy-start.5
  499.4 2.2 fusion.8
  501.6 0.0 copy-done.5
  501.6 2.2 fusion.10
  503.9 68.5 %reduce-scatter.7.cloned.1.call-done = f32[48,512]{1,0:T(8,128)} async-done(((f32[768,512]{1,0:T(8,128)}), f32[48,512]{1,0:T(8,128)}) %reduce-scatter.7.cloned.1.call-update) | async-done | bytes 98320 | tf_op jit(solution)/shard_map/reduce_scatter | solution.py:47
  572.4 80.4 %reduce-scatter.11.cloned.1.call-done = f32[48,512]{1,0:T(8,128)} async-done(((f32[768,512]{1,0:T(8,128)}), f32[48,512]{1,0:T(8,128)}) %reduce-scatter.11.cloned.1.call-update) | async-done | bytes 98320 | tf_op jit(solution)/shard_map/reduce_scatter | solution.py:57
Async XLA Ops:
  7.2 58.6 %copy-start = (bf16[896,512]{1,0:T(8,128)(2,1)S(1)}, bf16[896,512]{1,0:T(8,128)(2,1)}, u32[]{:S(2)}) copy-start(bf16[896,512]{1,0:T(8,128)(2,1)} %param.8) | copy-start | bytes 2752516
  7.2 58.6 %all-gather.5.cloned.1.call-start = ((), (), s32[]{:S(2)}) async-start(), calls=%async_computation.4 | async-start | bytes 1671168 | tf_op jit(solution)/shard_map/all_gather | solution.py:23
  8.8 138.1 %reduce-scatter.9.cloned.1.call-start = ((), (), s32[]{:S(2)}) async-start(), calls=%async_computation.8 | async-start | bytes 2924544 | tf_op jit(solution)/shard_map/reduce_scatter | solution.py:35
  69.4 1.2 copy-start.1
  69.4 1.7 copy-start.2
  69.5 205.0 %reduce-scatter.5.cloned.1.call-start = ((), (), s32[]{:S(2)}) async-start(), calls=%async_computation.5 | async-start | bytes 5849088 | tf_op jit(solution)/shard_map/reduce_scatter | solution.py:28
  76.3 270.1 %all-gather.7.cloned.1.call-start = ((), (), s32[]{:S(2)}) async-start(), calls=%async_computation.6 | async-start | bytes 1462272 | tf_op jit(solution)/shard_map/all_gather | solution.py:45
  276.4 142.3 %all-gather.9.cloned.1.call-start = ((), (), s32[]{:S(2)}) async-start(), calls=%async_computation.9 | async-start | bytes 1462272 | tf_op jit(solution)/shard_map/all_gather | solution.py:54
  277.0 213.9 %all-gather.11.cloned.1.call-start = ((), (), s32[]{:S(2)}) async-start(), calls=%async_computation.10 | async-start | bytes 1462272 | tf_op jit(solution)/shard_map/all_gather | solution.py:55
  277.5 294.8 %reduce-scatter.7.cloned.1.call-start = ((), (), s32[]{:S(2)}) async-start(), calls=%async_computation.7 | async-start | bytes 1671168 | tf_op jit(solution)/shard_map/reduce_scatter | solution.py:47
  349.9 302.8 %reduce-scatter.11.cloned.1.call-start = ((), (), s32[]{:S(2)}) async-start(), calls=%async_computation.11 | async-start | bytes 1671168 | tf_op jit(solution)/shard_map/reduce_scatter | solution.py:57
  494.4 1.4 copy-start.3
  495.8 3.6 copy-start.4
  499.4 2.2 copy-start.5
Sparse Core Ops, SparseCore 0:
  11.3 54.4 all-gather.4
  69.6 77.3 reduce-scatter.8
  149.7 124.7 reduce-scatter.4
  276.7 69.6 all-gather.6
  348.6 69.9 all-gather.8
  420.9 69.9 all-gather.10
  495.6 76.6 reduce-scatter.6
  577.1 75.5 reduce-scatter.10
